TPU v7x, 32 devices: a whole 2x2x4 slice. The times are simulated.
32 devices in a mesh: node: 8 (over z, x), local: 4 (over y, core).
Axes of the slice: x: 2, y: 2, z: 4, core: 2. Of those that a mesh axis runs over, the one named last changes fastest.
Arguments:
- tokens: bfloat16 [512, 7168], P('node'), may hold values from -6 to 6
- router_weight: bfloat16 [7168, 32], replicated, may hold values from -0.125 to 0.125
- expert_ids: int32 [512, 8], P('node'), may hold values from 0 to 31, as said below
- gate_weight: bfloat16 [32, 7168, 2048], P('node', None, 'local'), may hold values from -0.0625 to 0.0625
- up_weight: bfloat16 [32, 7168, 2048], P('node', None, 'local'), may hold values from -0.0625 to 0.0625
- down_weight: bfloat16 [32, 2048, 7168], P('node', 'local'), may hold values from -0.125 to 0.125
Outputs:
- combined: bfloat16 [512, 7168], P('node', 'local')
Inputs may be any that keep to these rules, and one draw needn't show every extreme that they name: `expert_ids`: each token names 8 different experts: two from each of 4 different groups of 4 consecutive experts (group e // 4), one from each half of the group (e // 2). Among the 64 tokens of one index of node, two groups are named by exactly 40 tokens, four by exactly 32 and two by exactly 24.
All inputs are finite; a program needn't handle non-finite values.
Results may differ from a plain program's by a relative error of at most 0.012.
Values may be sent and summed in bfloat16 or wider, within the bound.
A program may use at most 192 MiB of HBM per device.

v0:
```python
import jax
import jax.numpy as jnp
from jax import lax
from jax.sharding import PartitionSpec as P

D = 7168
EXPERTS = 32
CAP = 40


ROUTE_SCALE = 2.5


def body(tokens, router_weight, expert_ids, gate_weight, up_weight, down_weight):
    node_count = lax.axis_size("node")
    local_count = lax.axis_size("local")
    exp_node = gate_weight.shape[0]
    rows_dev = tokens.shape[0]
    capacity = CAP
    share = D // local_count
    scores = jax.nn.sigmoid(jnp.dot(tokens, router_weight, preferred_element_type=jnp.float32))
    picked = jnp.any(
        expert_ids[:, :, None] == jnp.arange(EXPERTS, dtype=jnp.int32)[None, None, :], axis=1
    )
    chosen_scores = jnp.where(picked, scores, 0.0)
    weights = (ROUTE_SCALE * chosen_scores / jnp.sum(chosen_scores, axis=1, keepdims=True)).astype(
        jnp.bfloat16
    )
    node_weights = weights.reshape(rows_dev, node_count, exp_node)
    reached = jnp.any(picked.reshape(rows_dev, node_count, exp_node), axis=2)
    slot_index = jnp.cumsum(reached.astype(jnp.int32), axis=0) - 1
    positions = jnp.arange(capacity, dtype=jnp.int32)[None, :, None]
    onehot = (reached.T[:, None, :] & (slot_index.T[:, None, :] == positions)).astype(jnp.bfloat16)
    send_weights = jnp.einsum(
        "mct,tme->mce", onehot, node_weights, preferred_element_type=jnp.float32
    ).astype(jnp.bfloat16)
    send_rows = jnp.einsum(
        "mct,td->mcd", onehot, tokens, preferred_element_type=jnp.float32
    ).astype(jnp.bfloat16)
    got_rows, got_weights = (
        lax.all_to_all(send_rows, "node", split_axis=0, concat_axis=0, tiled=True),
        lax.all_to_all(send_weights, "node", split_axis=0, concat_axis=0, tiled=True),
    )
    flat_rows = got_rows.reshape(-1, D)
    flat_weights = got_weights.reshape(-1, exp_node).astype(jnp.float32)
    gate_out = jnp.einsum("rd,edh->reh", flat_rows, gate_weight, preferred_element_type=jnp.float32)
    up_out = jnp.einsum("rd,edh->reh", flat_rows, up_weight, preferred_element_type=jnp.float32)
    hidden = (flat_weights[:, :, None] * jax.nn.silu(gate_out) * up_out).astype(jnp.bfloat16)
    partial_value = jnp.einsum(
        "reh,ehd->rd", hidden, down_weight, preferred_element_type=jnp.float32
    ).astype(jnp.bfloat16)
    pieces = partial_value.reshape(node_count, capacity, local_count, share)
    pieces = lax.all_to_all(
        lax.all_to_all(pieces, "node", split_axis=0, concat_axis=0, tiled=True),
        "local",
        split_axis=2,
        concat_axis=2,
        tiled=True,
    )
    node_out = jnp.sum(pieces.astype(jnp.float32), axis=2).astype(jnp.bfloat16)
    combined = jnp.einsum("mct,mcd->td", onehot, node_out, preferred_element_type=jnp.float32)
    return combined.astype(jnp.bfloat16)


def solution(mesh):
    return jax.shard_map(
        body,
        mesh=mesh,
        in_specs=(
            P("node", None),
            P(),
            P("node", None),
            P("node", None, "local"),
            P("node", None, "local"),
            P("node", "local", None),
        ),
        out_specs=P("node", "local"),
        check_vma=False,
    )
```

profile of v0, /device:TPU:0, one launch (start us, length us, event | category | flops | bytes accessed | tf_op | source)
XLA Modules:
  0.0 347.7 jit_solution(11950702859048186445)
XLA Ops:
  0.0 0.0 copy-start
  0.0 0.8 fusion.13
  0.8 0.1 copy.35
  0.9 0.1 reduce_window_sum.11
  1.0 0.1 copy.36
  1.1 0.1 copy-done
  1.2 1.4 fusion.21
  2.6 0.8 convolution_convert_fusion.1
  3.4 7.3 %all-to-all-start = ((bf16[8,40,4]{1,2,0:T(4,128)(2,1)}), bf16[8,40,4]{1,2,0:T(4,128)(2,1)S(1)}, u32[]{:S(2)}, u32[]{:S(2)}) async-start(bf16[8,40,4]{1,2,0:T(4,128)(2,1)} %convolution_convert_fusion.1), calls=%async_computation | async-start | bytes 16384 | tf_op jit(solution)/shard_map/all_to_all | solution.py:42
  10.6 3.5 %convolution_convert_fusion = bf16[8,40,7168]{2,1,0:T(8,128)(2,1)} fusion(bf16[64,7168]{1,0:T(8,128)(2,1)S(1)} %copy-done, s32[8,64]{1,0:T(8,128)S(1)} %copy.36, pred[8,64]{1,0:T(8,128)(4,1)S(1)} %bitcast.41), kind=kOutput, calls=%fused_computation.2 | convolution fusion | flops 295936000 | bytes 5507584 | tf_op jit(solution)/shard_map/mct,td->mcd/dot_general | solution.py:37
  14.1 3.0 all-to-all-done
  17.2 4.6 %all-to-all-start.1 = ((bf16[8,40,7168]{2,1,0:T(8,128)(2,1)}), bf16[8,40,7168]{2,1,0:T(8,128)(2,1)}, u32[]{:S(2)}, u32[]{:S(2)}) async-start(bf16[8,40,7168]{2,1,0:T(8,128)(2,1)} %convolution_convert_fusion), calls=%async_computation.1 | async-start | bytes 9175040 | tf_op jit(solution)/shard_map/all_to_all | solution.py:41
  21.8 0.1 reshape.28
  21.8 100.4 %all-to-all-done.1 = bf16[8,40,7168]{2,1,0:T(8,128)(2,1)} async-done(((bf16[8,40,7168]{2,1,0:T(8,128)(2,1)}), bf16[8,40,7168]{2,1,0:T(8,128)(2,1)}, u32[]{:S(2)}, u32[]{:S(2)}) %all-to-all-start.1) | async-done | bytes 4587552 | tf_op jit(solution)/shard_map/all_to_all | solution.py:41
  122.2 15.3 %fusion.22 = f32[320,4,512]{2,0,1:T(8,128)S(1)} fusion(bf16[320,7168,1]{1,0,2:T(8,128)(2,1)} %bitcast.6, bf16[4,7168,512]{2,1,0:T(8,128)(2,1)} %param.10), kind=kOutput, calls=%fused_computation.30 | convolution fusion | flops 9395240960 | bytes 36569088 | tf_op jit(solution)/shard_map/rd,edh->reh/dot_general | solution.py:47
  137.5 16.7 %multiply_convert_fusion.clone.4 = bf16[320,4,512]{2,0,1:T(8,128)(2,1)S(1)} fusion(f32[320,4,512]{2,0,1:T(8,128)S(1)} %fusion.22, bf16[320,7168,1]{1,0,2:T(8,128)(2,1)} %bitcast.6, bf16[4,7168,512]{2,1,0:T(8,128)(2,1)} %param.9, f32[320,4]{0,1:T(4,128)S(1)} %reshape.28), kind=kOutput, calls=%fused_computation.3.clone.clone.clone.1 | convolution fusion | flops 9399828480 | bytes 37884928 | tf_op jit(solution)/shard_map/rd,edh->reh/dot_general | solution.py:46
  154.2 16.4 %fusion = bf16[320,7168]{1,0:T(8,128)(2,1)} fusion(bf16[4,512,7168]{2,1,0:T(8,128)(2,1)} %param.11, bf16[320,4,512]{2,0,1:T(8,128)(2,1)S(1)} %multiply_convert_fusion.clone.4), kind=kOutput, calls=%fused_computation.1 | convolution fusion | flops 9397534720 | bytes 35258368 | tf_op jit(solution)/shard_map/reh,ehd->rd/dot_general | solution.py:49
  170.6 8.2 %reshape.27 = bf16[8,40,4,1792]{3,2,1,0:T(4,128)(2,1)} reshape(bf16[320,7168]{1,0:T(8,128)(2,1)} %fusion) | data formatting | bytes 9175040 | tf_op jit(solution)/shard_map/reshape | solution.py:52
  178.7 2.9 copy.38
  181.6 105.5 %all_to_all.20 = bf16[8,40,4,1792]{3,1,2,0:T(8,128)(2,1)S(1)} all-to-all(bf16[8,40,4,1792]{3,1,2,0:T(8,128)(2,1)S(1)} %copy.38), channel_id=1, replica_groups=mesh['node'=8,'local'=4] {'node'}, dimensions={0} | all-to-all | bytes 9175040 | tf_op jit(solution)/shard_map/all_to_all | solution.py:54
  287.2 0.3 copy.39
  287.5 0.0 copy-start.1
  287.5 56.0 %all_to_all.21 = bf16[8,40,4,1792]{3,1,0,2:T(8,128)(2,1)} all-to-all(bf16[8,40,4,1792]{3,1,0,2:T(8,128)(2,1)S(1)} %copy.39), channel_id=1, replica_groups=mesh['node'=8,'local'=4] {'local'}, dimensions={2} | all-to-all | bytes 9175040 | tf_op jit(solution)/shard_map/all_to_all | solution.py:53
  343.5 3.2 reduce_sum.22
  346.6 1.1 fusion.1
  347.7 0.0 copy-done.1
  (5 shorter events, 0.1 us)
Async XLA Ops:
  0.0 1.2 copy-start
  3.4 13.8 %all-to-all-start = ((bf16[8,40,4]{1,2,0:T(4,128)(2,1)}), bf16[8,40,4]{1,2,0:T(4,128)(2,1)S(1)}, u32[]{:S(2)}, u32[]{:S(2)}) async-start(bf16[8,40,4]{1,2,0:T(4,128)(2,1)} %convolution_convert_fusion.1), calls=%async_computation | async-start | bytes 16384 | tf_op jit(solution)/shard_map/all_to_all | solution.py:42
  17.2 105.0 %all-to-all-start.1 = ((bf16[8,40,7168]{2,1,0:T(8,128)(2,1)}), bf16[8,40,7168]{2,1,0:T(8,128)(2,1)}, u32[]{:S(2)}, u32[]{:S(2)}) async-start(bf16[8,40,7168]{2,1,0:T(8,128)(2,1)} %convolution_convert_fusion), calls=%async_computation.1 | async-start | bytes 9175040 | tf_op jit(solution)/shard_map/all_to_all | solution.py:41
  287.5 60.2 %copy-start.1 = (bf16[64,7168]{1,0:T(8,128)(2,1)S(1)}, bf16[64,7168]{1,0:T(8,128)(2,1)}, u32[]{:S(2)}) copy-start(bf16[64,7168]{1,0:T(8,128)(2,1)} %param.6) | copy-start | bytes 2752516
where the time goes:
time: 348 us
  blocking collectives  161 us (46%)
  waiting for transfers between devices  103 us (30%)
  matrix products  55.1 us (16%)
  starting transfers between devices  11.8 us (3%)
  local copies, waits for them, and re-layouts  11.7 us (3%)
  other arithmetic  4.11 us (1%)
    all_to_all x1, blocking collectives, body(): lax.all_to_all(pieces, 'node', split_axis=0, concat_axis=0, tiled=True)  106 us
    all_to_all x1, waiting for transfers between devices, body(): lax.all_to_all(send_rows, 'node', split_axis=0, concat_axis=0, tiled=True)  100 us
    all_to_all x1, blocking collectives, body(): lax.all_to_all(lax.all_to_all(pieces, 'node', split_axis=0, concat_axis=0...  56 us
    dot_general x1, matrix products, body(): jnp.einsum('rd,edh->reh', flat_rows, gate_weight, preferred_element_type=...  16.7 us
    dot_general x1, matrix products, body(): jnp.einsum('reh,ehd->rd', hidden, down_weight, preferred_element_type=jnp...  16.4 us
    dot_general x1, matrix products, body(): jnp.einsum('rd,edh->reh', flat_rows, up_weight, preferred_element_type=jn...  15.3 us
    reshape x2, local copies, waits for them, and re-layouts, body(): pieces = partial_value.reshape(node_count, capacity, local_count, share)  11.1 us
    all_to_all x1, starting transfers between devices, body(): lax.all_to_all(send_weights, 'node', split_axis=0, concat_axis=0, tiled=T...  7.25 us
  transfers between devices with their start and end apart: 2, of which 2 were waited for; matrix products, arithmetic and copies ran while one was open for 1% of the time, Pallas kernels for 0%

commit v1 on v0

v1 whole, which is shorter than its diff:
```python
import functools

import jax
import jax.numpy as jnp
from jax import lax
from jax.experimental import pallas as pl
from jax.experimental.pallas import tpu as pltpu
from jax.sharding import PartitionSpec as P

EXPERTS = 32
CAP = 40
ROUTE_SCALE = 2.5
MESH = pl.DeviceIdType.MESH
LANES = 128
PARTS = 7
LAG = 2


def place(nodes, locals_):
    me, l = lax.axis_index("node"), lax.axis_index("local")
    return me, l, lax.div(me, 2), lax.rem(me, 2), lax.div(l, 2), lax.rem(l, 2)


def greet(nodes, ys):
    me, l, z, x, y, c = place(nodes, ys * 2)
    barrier = pltpu.get_barrier_semaphore()
    for k in range(1, nodes):
        pl.semaphore_signal(
            barrier, inc=1, device_id=(lax.rem(me + k, nodes), l), device_id_type=MESH
        )
    for dy in range(1, ys):
        pl.semaphore_signal(
            barrier, inc=1, device_id=(me, lax.rem(y + dy, ys) * 2 + c), device_id_type=MESH
        )
    pl.semaphore_signal(barrier, inc=1, device_id=(me, y * 2 + 1 - c), device_id_type=MESH)
    pl.semaphore_wait(barrier, nodes - 1 + ys)


def remote(src, dst, send_sem, recv_sem, device):
    return pltpu.make_async_remote_copy(
        src_ref=src, dst_ref=dst, send_sem=send_sem, recv_sem=recv_sem,
        device_id=device, device_id_type=MESH,
    )


def dispatch_kernel(
    nodes, ys, slots,
    send, sendw, gate, up, hid,
    recv, recvw, rows, acc, wbuf,
    wsem, n_ss, n_rs, w_ss, w_rs, y_ss, y_rs, c_ss, c_rs,
):
    me, l, z, x, y, c = place(nodes, ys * 2)
    zs = nodes // 2
    pair = 2 * CAP
    experts = gate.shape[0]
    share = send.shape[2]
    tiles = 2 * ys * experts
    sib = (me, y * 2 + 1 - c)

    def quarter(qi):
        dy, dc = lax.div(qi, 2), lax.rem(qi, 2)
        return lax.rem(y + ys - dy, ys) * 2 + lax.rem(c + dc, 2)

    def fetch(t, slot):
        q = quarter(lax.div(t, experts))
        e = lax.rem(t, experts)
        at = pl.ds(pl.multiple_of(q * share, LANES), share)
        return (
            pltpu.make_async_copy(gate.at[e, at, :], wbuf.at[slot, 0], wsem.at[slot, 0]),
            pltpu.make_async_copy(up.at[e, at, :], wbuf.at[slot, 1], wsem.at[slot, 1]),
        )

    for t in range(min(slots, tiles)):
        for copy in fetch(jnp.int32(t), t):
            copy.start()

    greet(nodes, ys)

    def node_copies(dz, dx):
        m = lax.rem(z + dz, zs) * 2 + lax.rem(x + dx, 2)
        k = dz * 2 + dx
        return (
            remote(send.at[m], recv.at[me], n_ss.at[k], n_rs.at[k], (m, l)),
            remote(sendw.at[m], recvw.at[me], w_ss.at[k], w_rs.at[k], (m, l)),
        )

    def block(q, dz):
        zz = lax.rem(z + zs - dz, zs)
        return rows.at[q, pl.ds(pl.multiple_of(zz * pair, 16), pair), :]

    def y_copy(dz, dy):
        return remote(
            block(l, dz), block(l, dz), y_ss.at[dz, dy], y_rs.at[dz, dy],
            (me, lax.rem(y + dy, ys) * 2 + c),
        )

    def sib_copy(dz, dy):
        q = lax.rem(y + ys - dy, ys) * 2 + c
        return remote(block(q, dz), block(q, dz), c_ss.at[dz, dy], c_rs.at[dz, dy], sib)

    for dz in range(zs):
        for dx in range(2):
            if dz + dx > 0:
                for copy in node_copies(dz, dx):
                    copy.start()
    recv[me] = send[me]
    recvw[me] = sendw[me]

    def forward(dz):
        for dy in range(1, ys):
            y_copy(dz, dy).wait_recv()
            sib_copy(dz, dy).start()

    for dz in range(zs):
        for dx in range(2):
            if dz + dx > 0:
                for copy in node_copies(dz, dx):
                    copy.wait_recv()
        zz = lax.rem(z + zs - dz, zs)
        got = recv[pl.ds(zz * 2, 2)].astype(jnp.float32).reshape(pair, share)
        rows[l, pl.ds(pl.multiple_of(zz * pair, 16), pair), :] = got.astype(jnp.bfloat16)
        for dy in range(1, ys):
            y_copy(dz, dy).start()
        sib_copy(dz, 0).start()
        if dz > 0:
            forward(dz - 1)

    for qi in range(2 * ys):
        dy, dc = qi // 2, qi % 2
        if qi == 1:
            forward(zs - 1)
        if dc == 1:
            for dz in range(zs):
                sib_copy(dz, dy).wait_recv()
        q = quarter(jnp.int32(qi))

        def step(e, carry):
            t = qi * experts + e
            slot = lax.rem(t, slots)
            for copy in fetch(t, slot):
                copy.wait()
            for g in range(2):
                part = jnp.dot(rows[q], wbuf[slot, g], preferred_element_type=jnp.float32)
                if qi == 0:
                    acc[e, g] = part
                else:
                    acc[e, g] += part

            @pl.when(t + slots < tiles)
            def _():
                for copy in fetch(t + slots, slot):
                    copy.start()

            return carry

        lax.fori_loop(0, experts, step, 0)

    gain = recvw[...].astype(jnp.float32).reshape(nodes * CAP, LANES)
    width = gate.shape[2]
    for e in range(experts):
        v = acc[e, 0]
        value = gain[:, e:e + 1] * (v / (1.0 + jnp.exp(-v))) * acc[e, 1]
        hid[:, e * width:(e + 1) * width] = value.astype(jnp.bfloat16)

    for dz in range(zs):
        for dx in range(2):
            if dz + dx > 0:
                for copy in node_copies(dz, dx):
                    copy.wait_send()
        for dy in range(ys):
            if dy > 0:
                y_copy(dz, dy).wait_send()
            sib_copy(dz, dy).wait_send()


def combine_kernel(
    nodes, ys,
    hid, down, back, out,
    wbuf, own, psib, gsib, psum, gsum, pnode, gnode,
    wsem, c_ss, c_rs, y_ss, y_rs, n_ss, n_rs,
):
    me, l, z, x, y, c = place(nodes, ys * 2)
    share = out.shape[1]
    width = share // PARTS
    sib = (me, y * 2 + 1 - c)

    def fetch(f, d, dc):
        q = lax.rem(y + d + 1, ys) * 2 + lax.rem(c + dc, 2)
        at = pl.ds(pl.multiple_of(q * share + f * width, LANES), width)
        return pltpu.make_async_copy(down.at[:, at], wbuf.at[f, d, dc], wsem.at[f, d, dc])

    def start_weights(f, carry):
        for d in range(ys):
            for dc in (1, 0):
                fetch(f, d, dc).start()
        return carry

    lax.fori_loop(0, PARTS, start_weights, 0)
    greet(nodes, ys)

    def sib_copy(f, d):
        return remote(psib.at[f, d], gsib.at[f, d], c_ss.at[f, d], c_rs.at[f, d], sib)

    def y_copy(f, d):
        to = (me, lax.rem(y + d + 1, ys) * 2 + c)
        return remote(psum.at[f, d], gsum.at[f, d], y_ss.at[f, d], y_rs.at[f, d], to)

    def node_copy(f, k):
        m = lax.rem(me + k, nodes)
        return remote(pnode.at[f, m], gnode.at[f, me], n_ss.at[f, k], n_rs.at[f, k], (m, l))

    def step(f, carry):
        @pl.when(f < PARTS)
        def _():
            for d in range(ys):
                fetch(f, d, 1).wait()
                part = jnp.dot(hid[...], wbuf[f, d, 1], preferred_element_type=jnp.float32)
                psib[f, d] = part.astype(jnp.bfloat16)
                sib_copy(f, d).start()
                fetch(f, d, 0).wait()
                own[f, d] = jnp.dot(hid[...], wbuf[f, d, 0], preferred_element_type=jnp.float32)
            for d in range(ys - 1):
                sib_copy(f, d).wait_recv()
                psum[f, d] = (own[f, d] + gsib[f, d].astype(jnp.float32)).astype(jnp.bfloat16)
                y_copy(f, d).start()

        @pl.when(f >= LAG)
        def _():
            g = f - LAG
            sib_copy(g, ys - 1).wait_recv()
            total = own[g, ys - 1] + gsib[g, ys - 1].astype(jnp.float32)
            for d in range(ys - 1):
                y_copy(g, d).wait_recv()
                total += gsum[g, d].astype(jnp.float32)
            pnode[g] = total.reshape(nodes, CAP, width).astype(jnp.bfloat16)
            for k in range(1, nodes):
                node_copy(g, k).start()
            gnode[g, me] = pnode[g, me]

        return carry

    lax.fori_loop(0, PARTS + LAG, step, 0)

    def finish(f, carry):
        for k in range(1, nodes):
            node_copy(f, k).wait_recv()
        got = gnode[f].astype(jnp.float32).reshape(nodes * CAP, width).astype(jnp.bfloat16)
        at = pl.ds(pl.multiple_of(f * width, LANES), width)
        out[:, at] = jnp.dot(back[...], got, preferred_element_type=jnp.float32).astype(jnp.bfloat16)
        return carry

    lax.fori_loop(0, PARTS, finish, 0)

    def drain(f, carry):
        for d in range(ys):
            sib_copy(f, d).wait_send()
            if d < ys - 1:
                y_copy(f, d).wait_send()
        for k in range(1, nodes):
            node_copy(f, k).wait_send()
        return carry

    lax.fori_loop(0, PARTS, drain, 0)


def body(tokens, router_weight, expert_ids, gate_weight, up_weight, down_weight):
    nodes = lax.axis_size("node")
    locals_ = lax.axis_size("local")
    ys, zs = locals_ // 2, nodes // 2
    experts, dim, hid_dev = gate_weight.shape
    rows_dev = tokens.shape[0]
    share = dim // locals_
    total_rows = nodes * CAP
    bf16, f32 = jnp.bfloat16, jnp.float32
    scores = jax.nn.sigmoid(jnp.dot(tokens, router_weight, preferred_element_type=f32))
    picked = jnp.any(
        expert_ids[:, :, None] == jnp.arange(EXPERTS, dtype=jnp.int32)[None, None, :], axis=1
    )
    chosen = jnp.where(picked, scores, 0.0)
    weights = (ROUTE_SCALE * chosen / jnp.sum(chosen, axis=1, keepdims=True)).astype(bf16)
    node_weights = weights.reshape(rows_dev, nodes, experts)
    reached = jnp.any(picked.reshape(rows_dev, nodes, experts), axis=2)
    slot_index = jnp.cumsum(reached.astype(jnp.int32), axis=0) - 1
    positions = jnp.arange(CAP, dtype=jnp.int32)[None, :, None]
    onehot = (reached.T[:, None, :] & (slot_index.T[:, None, :] == positions)).astype(bf16)
    send_w = jnp.einsum(
        "mct,tme->mce", onehot, node_weights, preferred_element_type=f32
    ).astype(bf16)
    send_w = jnp.pad(send_w, ((0, 0), (0, 0), (0, LANES - experts)))
    mine = lax.dynamic_slice_in_dim(tokens, lax.axis_index("local") * share, share, 1)
    send = jnp.einsum("mct,td->mcd", onehot, mine, preferred_element_type=f32).astype(bf16)
    back = onehot.transpose(2, 0, 1).reshape(rows_dev, total_rows)

    vmem = pl.BlockSpec(memory_space=pltpu.VMEM)
    hbm = pl.BlockSpec(memory_space=pl.ANY)
    dma = pltpu.SemaphoreType.DMA
    tiles = locals_ * experts
    slots = min(tiles, 10)
    hidden = pl.pallas_call(
        functools.partial(dispatch_kernel, nodes, ys, slots),
        out_shape=jax.ShapeDtypeStruct((total_rows, experts * hid_dev), bf16),
        in_specs=[vmem, vmem, hbm, hbm],
        out_specs=vmem,
        scratch_shapes=[
            pltpu.VMEM((nodes, CAP, share), bf16),
            pltpu.VMEM((nodes, CAP, LANES), bf16),
            pltpu.VMEM((locals_, total_rows, share), bf16),
            pltpu.VMEM((experts, 2, total_rows, hid_dev), f32),
            pltpu.VMEM((slots, 2, share, hid_dev), bf16),
            dma((slots, 2)),
            dma((nodes,)), dma((nodes,)), dma((nodes,)), dma((nodes,)),
            dma((zs, ys)), dma((zs, ys)), dma((zs, ys)), dma((zs, ys)),
        ],
        compiler_params=pltpu.CompilerParams(
            collective_id=0, has_side_effects=True, vmem_limit_bytes=58 * 2**20
        ),
        cost_estimate=pl.CostEstimate(
            flops=4 * total_rows * dim * experts * hid_dev,
            bytes_accessed=4 * experts * dim * hid_dev,
            transcendentals=total_rows * experts * hid_dev,
        ),
    )(send, send_w, gate_weight, up_weight)

    width = share // PARTS
    return pl.pallas_call(
        functools.partial(combine_kernel, nodes, ys),
        out_shape=jax.ShapeDtypeStruct((rows_dev, share), bf16),
        in_specs=[vmem, hbm, vmem],
        out_specs=vmem,
        scratch_shapes=[
            pltpu.VMEM((PARTS, ys, 2, experts * hid_dev, width), bf16),
            pltpu.VMEM((PARTS, ys, total_rows, width), f32),
            pltpu.VMEM((PARTS, ys, total_rows, width), bf16),
            pltpu.VMEM((PARTS, ys, total_rows, width), bf16),
            pltpu.VMEM((PARTS, ys - 1, total_rows, width), bf16),
            pltpu.VMEM((PARTS, ys - 1, total_rows, width), bf16),
            pltpu.VMEM((PARTS, nodes, CAP, width), bf16),
            pltpu.VMEM((PARTS, nodes, CAP, width), bf16),
            dma((PARTS, ys, 2)),
            dma((PARTS, ys)), dma((PARTS, ys)),
            dma((PARTS, ys)), dma((PARTS, ys)),
            dma((PARTS, nodes)), dma((PARTS, nodes)),
        ],
        compiler_params=pltpu.CompilerParams(
            collective_id=1, has_side_effects=True, vmem_limit_bytes=58 * 2**20
        ),
        cost_estimate=pl.CostEstimate(
            flops=2 * total_rows * dim * experts * hid_dev,
            bytes_accessed=2 * experts * dim * hid_dev,
            transcendentals=0,
        ),
    )(hidden, down_weight.reshape(experts * hid_dev, dim), back)


def solution(mesh):
    return jax.shard_map(
        body,
        mesh=mesh,
        in_specs=(
            P("node", None),
            P(),
            P("node", None),
            P("node", None, "local"),
            P("node", None, "local"),
            P("node", "local", None),
        ),
        out_specs=P("node", "local"),
        check_vma=False,
    )
```

time: 348 us -> 118 us (0.34)
  blocking collectives: 161 us -> 0 us
  Pallas kernels: 0 us -> 110 us
  waiting for transfers between devices: 103 us -> 0 us
  matrix products: 55.1 us -> 3.02 us
  starting transfers between devices: 11.8 us -> 0 us
  local copies, waits for them, and re-layouts: 11.7 us -> 3.15 us
    all_to_all x2 -> x0, blocking collectives: 161 us -> none  [the longest x1 106 us: body(): lax.all_to_all(pieces, 'node', split_axis=0, concat_axis=0, tiled=True)]
    pallas_call x0 -> x2, Pallas kernels: none -> 110 us  [the longest x1 62.2 us: body(): pl.pallas_call(functools.partial(dispatch_kernel, nodes, ys, slots), out_...]
    all_to_all x2 -> x0, waiting for transfers between devices: 103 us -> none  [the longest x1 100 us: body(): lax.all_to_all(send_rows, 'node', split_axis=0, concat_axis=0, tiled=True)]
    dot_general x7 -> x3, matrix products: 55.1 us -> 3.02 us  [the longest x1 1.45 us: body(): jnp.einsum('mct,td->mcd', onehot, mine, preferred_element_type=f32)]
    all_to_all x2 -> x0, starting transfers between devices: 11.8 us -> none  [the longest x1 7.25 us: body(): lax.all_to_all(send_weights, 'node', split_axis=0, concat_axis=0, tiled=T...]
    reshape x2 -> x0, local copies, waits for them, and re-layouts: 11.1 us -> none  [body(): pieces = partial_value.reshape(node_count, capacity, local_count, share)]
  transfers between devices with their start and end apart: 2 -> 0, of which waited for: 2 -> 0; matrix products, arithmetic and copies ran while one was open for 1% -> 0% of each run, Pallas kernels for 0% -> 0%
where the time goes in v1:
time: 118 us
  Pallas kernels  110 us (93%)
  local copies, waits for them, and re-layouts  3.15 us (3%)
  matrix products  3.02 us (3%)
  other arithmetic  1.59 us (1%)
    pallas_call x1, Pallas kernels, body(): pl.pallas_call(functools.partial(dispatch_kernel, nodes, ys, slots), out_...  62.2 us
    pallas_call x1, Pallas kernels, body(): pl.pallas_call(functools.partial(combine_kernel, nodes, ys), out_shape=ja...  48.1 us

profile of v1, /device:TPU:0, one launch (start us, length us, event | category | flops | bytes accessed | tf_op | source)
XLA Modules:
  0.0 118.1 jit_solution(2852345708975784383)
XLA Ops:
  0.0 0.0 copy-start
  0.0 0.8 fusion.10
  0.8 0.1 copy.32
  0.9 0.1 reduce_window_sum.11
  1.0 0.1 copy.33
  1.1 0.1 copy-done
  1.2 1.4 %convolution_convert_fusion.send = bf16[8,40,1792]{2,1,0:T(8,128)(2,1)} fusion(bf16[64,7168]{1,0:T(8,128)(2,1)S(1)} %copy-done, s32[]{:T(128)S(6)} %select_n.7, s32[8,64]{1,0:T(8,128)S(1)} %copy.33, pred[8,64]{1,0:T(8,128)(4,1)S(1)} %bitcast.17), kind=kOutput, calls=%fused_computation | convolution fusion | flops 74014720 | bytes 1381380 | tf_op jit(solution)/shard_map/mct,td->mcd/dot_general | solution.py:291
  2.6 1.4 %fusion.17 = (f32[64]{0:T(128)S(1)}, f32[64,32]{0,1:T(8,128)S(1)}) fusion(pred[64,32]{0,1:T(8,128)(4,1)S(1)} %fusion.10, bf16[64,7168]{1,0:T(8,128)(2,1)S(1)} %copy-done, bf16[7168,32]{0,1:T(8,128)(2,1)} %param.7), kind=kOutput, calls=%fused_computation.23 | convolution fusion | flops 29370304 | bytes 1386752 | tf_op jit(solution)/shard_map/dot_general | solution.py:275
  4.1 0.2 fusion.7
  4.2 0.2 copy.35
  4.4 0.7 pad.4.sendw
  5.1 62.2 %shard_map.64.hid = bf16[320,2048]{1,0:T(8,128)(2,1)} custom-call(bf16[8,40,1792]{2,1,0:T(8,128)(2,1)} %convolution_convert_fusion.send, bf16[8,40,128]{2,1,0:T(8,128)(2,1)} %pad.4.sendw, bf16[4,7168,512]{2,1,0:T(8,128)(2,1)} %gate.1, bf16[4,7168,512]{2,1,0:T(8,128)(2,1)} %up.1), custom_call_target="tpu_custom_call" | custom-call | flops 18790481920 | bytes 58720256 | tf_op jit(solution)/shard_map/pallas_call | solution.py:299
  67.3 0.1 copy.36
  67.4 0.1 copy.37
  67.5 0.1 copy.38
  67.6 0.1 eq.49
  67.7 0.7 and_convert_fusion.back
  68.4 0.0 copy-start.1
  68.4 48.1 %shard_map.65 = bf16[64,1792]{1,0:T(8,128)(2,1)} custom-call(bf16[320,2048]{1,0:T(8,128)(2,1)} %shard_map.64.hid, bf16[2048,7168]{1,0:T(8,128)(2,1)} %bitcast.20, bf16[64,320]{1,0:T(8,128)(2,1)} %and_convert_fusion.back), custom_call_target="tpu_custom_call" | custom-call | flops 9395240960 | bytes 29360128 | tf_op jit(solution)/shard_map/pallas_call | solution.py:325
  116.5 1.6 %copy.42 = bf16[64,1792]{1,0:T(8,128)(2,1)} copy(bf16[64,1792]{1,0:T(8,128)(2,1)} %shard_map.65) | data formatting | bytes 458752
  118.1 0.0 copy-done.1
  (8 shorter events, 0.1 us)
Async XLA Ops:
  0.0 1.2 %copy-start = (bf16[64,7168]{1,0:T(8,128)(2,1)S(1)}, bf16[64,7168]{1,0:T(8,128)(2,1)}, u32[]{:S(2)}) copy-start(bf16[64,7168]{1,0:T(8,128)(2,1)} %param.6) | copy-start | bytes 2752516
  68.4 49.7 %copy-start.1 = (bf16[64,7168]{1,0:T(8,128)(2,1)S(1)}, bf16[64,7168]{1,0:T(8,128)(2,1)}, u32[]{:S(2)}) copy-start(bf16[64,7168]{1,0:T(8,128)(2,1)} %param.6) | copy-start | bytes 2752516

commit v2 on v1

--- a/solution.py
+++ b/solution.py
@@ -13,6 +13,7 @@
 MESH = pl.DeviceIdType.MESH
 LANES = 128
 PARTS = 7
+WINDOW = 3
 LAG = 2
 
 
@@ -50,127 +51,136 @@
     wsem, n_ss, n_rs, w_ss, w_rs, y_ss, y_rs, c_ss, c_rs,
 ):
     me, l, z, x, y, c = place(nodes, ys * 2)
-    zs = nodes // 2
-    pair = 2 * CAP
-    experts = gate.shape[0]
-    share = send.shape[2]
-    tiles = 2 * ys * experts
+    total = nodes * CAP
+    experts, locals_, _, width, units = gate.shape
+    tiles = PARTS * experts
     sib = (me, y * 2 + 1 - c)
 
-    def quarter(qi):
-        dy, dc = lax.div(qi, 2), lax.rem(qi, 2)
-        return lax.rem(y + ys - dy, ys) * 2 + lax.rem(c + dc, 2)
-
     def fetch(t, slot):
-        q = quarter(lax.div(t, experts))
-        e = lax.rem(t, experts)
-        at = pl.ds(pl.multiple_of(q * share, LANES), share)
+        h, e = lax.div(t, experts), lax.rem(t, experts)
         return (
-            pltpu.make_async_copy(gate.at[e, at, :], wbuf.at[slot, 0], wsem.at[slot, 0]),
-            pltpu.make_async_copy(up.at[e, at, :], wbuf.at[slot, 1], wsem.at[slot, 1]),
+            pltpu.make_async_copy(
+                gate.at[e, :, h], wbuf.at[slot, :, :, :units], wsem.at[slot, 0]
+            ),
+            pltpu.make_async_copy(
+                up.at[e, :, h], wbuf.at[slot, :, :, units:], wsem.at[slot, 1]
+            ),
         )
 
-    for t in range(min(slots, tiles)):
-        for copy in fetch(jnp.int32(t), t):
+    def first(t, carry):
+        for copy in fetch(t, t):
             copy.start()
-
+        return carry
+
+    lax.fori_loop(0, slots, first, 0)
     greet(nodes, ys)
 
-    def node_copies(dz, dx):
-        m = lax.rem(z + dz, zs) * 2 + lax.rem(x + dx, 2)
-        k = dz * 2 + dx
-        return (
-            remote(send.at[m], recv.at[me], n_ss.at[k], n_rs.at[k], (m, l)),
-            remote(sendw.at[m], recvw.at[me], w_ss.at[k], w_rs.at[k], (m, l)),
+    def node_copy(h, k):
+        m = lax.rem(me + k, nodes)
+        at = pl.ds(pl.multiple_of(h * width, LANES), width)
+        return remote(
+            send.at[m, :, at], recv.at[h, me], n_ss.at[h, k], n_rs.at[h, k], (m, l)
         )
 
-    def block(q, dz):
-        zz = lax.rem(z + zs - dz, zs)
-        return rows.at[q, pl.ds(pl.multiple_of(zz * pair, 16), pair), :]
-
-    def y_copy(dz, dy):
-        return remote(
-            block(l, dz), block(l, dz), y_ss.at[dz, dy], y_rs.at[dz, dy],
-            (me, lax.rem(y + dy, ys) * 2 + c),
-        )
-
-    def sib_copy(dz, dy):
+    def gain_copy(k):
+        m = lax.rem(me + k, nodes)
+        return remote(sendw.at[m], recvw.at[me], w_ss.at[k], w_rs.at[k], (m, l))
+
+    def block(h, q):
+        return rows.at[h, :, pl.ds(pl.multiple_of(q * width, LANES), width)]
+
+    def y_copy(h, dy):
+        to = (me, lax.rem(y + dy, ys) * 2 + c)
+        return remote(block(h, l), block(h, l), y_ss.at[h, dy], y_rs.at[h, dy], to)
+
+    def sib_copy(h, dy):
         q = lax.rem(y + ys - dy, ys) * 2 + c
-        return remote(block(q, dz), block(q, dz), c_ss.at[dz, dy], c_rs.at[dz, dy], sib)
-
-    for dz in range(zs):
-        for dx in range(2):
-            if dz + dx > 0:
-                for copy in node_copies(dz, dx):
-                    copy.start()
-    recv[me] = send[me]
+        return remote(block(h, q), block(h, q), c_ss.at[h, dy], c_rs.at[h, dy], sib)
+
+    def send_all(h, carry):
+        for k in range(1, nodes):
+            node_copy(h, k).start()
+        at = pl.ds(pl.multiple_of(h * width, LANES), width)
+        recv[h, me] = send[me, :, at]
+        return carry
+
+    lax.fori_loop(0, WINDOW, send_all, 0)
+    for k in range(1, nodes):
+        gain_copy(k).start()
     recvw[me] = sendw[me]
-
-    def forward(dz):
-        for dy in range(1, ys):
-            y_copy(dz, dy).wait_recv()
-            sib_copy(dz, dy).start()
-
-    for dz in range(zs):
-        for dx in range(2):
-            if dz + dx > 0:
-                for copy in node_copies(dz, dx):
-                    copy.wait_recv()
-        zz = lax.rem(z + zs - dz, zs)
-        got = recv[pl.ds(zz * 2, 2)].astype(jnp.float32).reshape(pair, share)
-        rows[l, pl.ds(pl.multiple_of(zz * pair, 16), pair), :] = got.astype(jnp.bfloat16)
-        for dy in range(1, ys):
-            y_copy(dz, dy).start()
-        sib_copy(dz, 0).start()
-        if dz > 0:
-            forward(dz - 1)
-
-    for qi in range(2 * ys):
-        dy, dc = qi // 2, qi % 2
-        if qi == 1:
-            forward(zs - 1)
-        if dc == 1:
-            for dz in range(zs):
-                sib_copy(dz, dy).wait_recv()
-        q = quarter(jnp.int32(qi))
-
-        def step(e, carry):
-            t = qi * experts + e
-            slot = lax.rem(t, slots)
-            for copy in fetch(t, slot):
-                copy.wait()
-            for g in range(2):
-                part = jnp.dot(rows[q], wbuf[slot, g], preferred_element_type=jnp.float32)
-                if qi == 0:
-                    acc[e, g] = part
-                else:
-                    acc[e, g] += part
-
-            @pl.when(t + slots < tiles)
+    acc[...] = jnp.zeros(acc.shape, jnp.float32)
+
+    def step(i, carry):
+        @pl.when(i < PARTS)
+        def _():
+            for k in range(1, nodes):
+                node_copy(i, k).wait_recv()
+            got = recv[i].astype(jnp.float32).reshape(total, width)
+            at = pl.ds(pl.multiple_of(l * width, LANES), width)
+            rows[i, :, at] = got.astype(jnp.bfloat16)
+            for dy in range(1, ys):
+                y_copy(i, dy).start()
+            sib_copy(i, 0).start()
+
+            @pl.when(i + WINDOW < PARTS)
             def _():
-                for copy in fetch(t + slots, slot):
-                    copy.start()
-
-            return carry
-
-        lax.fori_loop(0, experts, step, 0)
-
-    gain = recvw[...].astype(jnp.float32).reshape(nodes * CAP, LANES)
-    width = gate.shape[2]
+                send_all(i + WINDOW, 0)
+
+        @pl.when((i >= 1) & (i <= PARTS))
+        def _():
+            for dy in range(1, ys):
+                y_copy(i - 1, dy).wait_recv()
+                sib_copy(i - 1, dy).start()
+
+        @pl.when(i >= 2)
+        def _():
+            h = i - 2
+            for dy in range(ys):
+                sib_copy(h, dy).wait_recv()
+
+            def expert(e, carry):
+                t = h * experts + e
+                slot = lax.rem(t, slots)
+                for copy in fetch(t, slot):
+                    copy.wait()
+                acc[e] += jnp.dot(
+                    rows[h], wbuf[slot].reshape(locals_ * width, 2 * units),
+                    preferred_element_type=jnp.float32,
+                )
+
+                @pl.when(t + slots < tiles)
+                def _():
+                    for copy in fetch(t + slots, slot):
+                        copy.start()
+
+                return carry
+
+            lax.fori_loop(0, experts, expert, 0)
+
+        return carry
+
+    lax.fori_loop(0, PARTS + 2, step, 0)
+
+    for k in range(1, nodes):
+        gain_copy(k).wait_recv()
+    gain = recvw[...].astype(jnp.float32).reshape(total, LANES)
     for e in range(experts):
-        v = acc[e, 0]
-        value = gain[:, e:e + 1] * (v / (1.0 + jnp.exp(-v))) * acc[e, 1]
-        hid[:, e * width:(e + 1) * width] = value.astype(jnp.bfloat16)
-
-    for dz in range(zs):
-        for dx in range(2):
-            if dz + dx > 0:
-                for copy in node_copies(dz, dx):
-                    copy.wait_send()
+        v = acc[e, :, :units]
+        value = gain[:, e:e + 1] * (v / (1.0 + jnp.exp(-v))) * acc[e, :, units:]
+        hid[:, e * units:(e + 1) * units] = value.astype(jnp.bfloat16)
+
+    def drain(h, carry):
+        for k in range(1, nodes):
+            node_copy(h, k).wait_send()
         for dy in range(ys):
             if dy > 0:
-                y_copy(dz, dy).wait_send()
-            sib_copy(dz, dy).wait_send()
+                y_copy(h, dy).wait_send()
+            sib_copy(h, dy).wait_send()
+        return carry
+
+    lax.fori_loop(0, PARTS, drain, 0)
+    for k in range(1, nodes):
+        gain_copy(k).wait_send()
 
 
 def combine_kernel(
@@ -187,7 +197,8 @@
     def fetch(f, d, dc):
         q = lax.rem(y + d + 1, ys) * 2 + lax.rem(c + dc, 2)
         at = pl.ds(pl.multiple_of(q * share + f * width, LANES), width)
-        return pltpu.make_async_copy(down.at[:, at], wbuf.at[f, d, dc], wsem.at[f, d, dc])
+        half = wbuf.at[f, d, :, (1 - dc) * width:(2 - dc) * width]
+        return pltpu.make_async_copy(down.at[:, at], half, wsem.at[f, d, dc])
 
     def start_weights(f, carry):
         for d in range(ys):
@@ -214,11 +225,11 @@
         def _():
             for d in range(ys):
                 fetch(f, d, 1).wait()
-                part = jnp.dot(hid[...], wbuf[f, d, 1], preferred_element_type=jnp.float32)
-                psib[f, d] = part.astype(jnp.bfloat16)
+                fetch(f, d, 0).wait()
+                part = jnp.dot(hid[...], wbuf[f, d], preferred_element_type=jnp.float32)
+                psib[f, d] = part[:, :width].astype(jnp.bfloat16)
                 sib_copy(f, d).start()
-                fetch(f, d, 0).wait()
-                own[f, d] = jnp.dot(hid[...], wbuf[f, d, 0], preferred_element_type=jnp.float32)
+                own[f, d] = part[:, width:]
             for d in range(ys - 1):
                 sib_copy(f, d).wait_recv()
                 psum[f, d] = (own[f, d] + gsib[f, d].astype(jnp.float32)).astype(jnp.bfloat16)
@@ -266,7 +277,7 @@
 def body(tokens, router_weight, expert_ids, gate_weight, up_weight, down_weight):
     nodes = lax.axis_size("node")
     locals_ = lax.axis_size("local")
-    ys, zs = locals_ // 2, nodes // 2
+    ys = locals_ // 2
     experts, dim, hid_dev = gate_weight.shape
     rows_dev = tokens.shape[0]
     share = dim // locals_
@@ -294,22 +305,23 @@
     vmem = pl.BlockSpec(memory_space=pltpu.VMEM)
     hbm = pl.BlockSpec(memory_space=pl.ANY)
     dma = pltpu.SemaphoreType.DMA
-    tiles = locals_ * experts
-    slots = min(tiles, 10)
+    width = share // PARTS
+    slots = min(PARTS * experts, 18)
+    pieces = (experts, locals_, PARTS, width, hid_dev)
     hidden = pl.pallas_call(
         functools.partial(dispatch_kernel, nodes, ys, slots),
         out_shape=jax.ShapeDtypeStruct((total_rows, experts * hid_dev), bf16),
         in_specs=[vmem, vmem, hbm, hbm],
         out_specs=vmem,
         scratch_shapes=[
-            pltpu.VMEM((nodes, CAP, share), bf16),
+            pltpu.VMEM((PARTS, nodes, CAP, width), bf16),
             pltpu.VMEM((nodes, CAP, LANES), bf16),
-            pltpu.VMEM((locals_, total_rows, share), bf16),
-            pltpu.VMEM((experts, 2, total_rows, hid_dev), f32),
-            pltpu.VMEM((slots, 2, share, hid_dev), bf16),
+            pltpu.VMEM((PARTS, total_rows, locals_ * width), bf16),
+            pltpu.VMEM((experts, total_rows, 2 * hid_dev), f32),
+            pltpu.VMEM((slots, locals_, width, 2 * hid_dev), bf16),
             dma((slots, 2)),
-            dma((nodes,)), dma((nodes,)), dma((nodes,)), dma((nodes,)),
-            dma((zs, ys)), dma((zs, ys)), dma((zs, ys)), dma((zs, ys)),
+            dma((PARTS, nodes)), dma((PARTS, nodes)), dma((nodes,)), dma((nodes,)),
+            dma((PARTS, ys)), dma((PARTS, ys)), dma((PARTS, ys)), dma((PARTS, ys)),
         ],
         compiler_params=pltpu.CompilerParams(
             collective_id=0, has_side_effects=True, vmem_limit_bytes=58 * 2**20
@@ -319,16 +331,15 @@
             bytes_accessed=4 * experts * dim * hid_dev,
             transcendentals=total_rows * experts * hid_dev,
         ),
-    )(send, send_w, gate_weight, up_weight)
-
-    width = share // PARTS
+    )(send, send_w, gate_weight.reshape(pieces), up_weight.reshape(pieces))
+
     return pl.pallas_call(
         functools.partial(combine_kernel, nodes, ys),
         out_shape=jax.ShapeDtypeStruct((rows_dev, share), bf16),
         in_specs=[vmem, hbm, vmem],
         out_specs=vmem,
         scratch_shapes=[
-            pltpu.VMEM((PARTS, ys, 2, experts * hid_dev, width), bf16),
+            pltpu.VMEM((PARTS, ys, experts * hid_dev, 2 * width), bf16),
             pltpu.VMEM((PARTS, ys, total_rows, width), f32),
             pltpu.VMEM((PARTS, ys, total_rows, width), bf16),
             pltpu.VMEM((PARTS, ys, total_rows, width), bf16),

time: 118 us -> 108 us (0.915)
  Pallas kernels: 110 us -> 99.5 us
    pallas_call x1, Pallas kernels: 62.2 us -> 53.6 us  [body(): pl.pallas_call(functools.partial(dispatch_kernel, nodes, ys, slots), out_...]
    pallas_call x1, Pallas kernels: 48.1 us -> 45.9 us  [body(): pl.pallas_call(functools.partial(combine_kernel, nodes, ys), out_shape=ja...]
where the time goes in v2:
time: 108 us; the launch traced here: 107 us
  Pallas kernels  99.5 us (92%)
  local copies, waits for them, and re-layouts  3.15 us (3%)
  matrix products  3.02 us (3%)
  other arithmetic  1.59 us (1%)
    pallas_call x1, Pallas kernels, body(): pl.pallas_call(functools.partial(dispatch_kernel, nodes, ys, slots), out_...  53.6 us
    pallas_call x1, Pallas kernels, body(): pl.pallas_call(functools.partial(combine_kernel, nodes, ys), out_shape=ja...  45.9 us

profile of v2, /device:TPU:0, one launch (start us, length us, event | category | flops | bytes accessed | tf_op | source)
XLA Modules:
  0.0 107.4 jit_solution(5700060085494961149)
XLA Ops:
  0.0 0.0 copy-start
  0.0 0.8 fusion.10
  0.8 0.1 copy.32
  0.9 0.1 reduce_window_sum.11
  1.0 0.1 copy.33
  1.1 0.1 copy-done
  1.2 1.4 %convolution_convert_fusion.send = bf16[8,40,1792]{2,1,0:T(8,128)(2,1)} fusion(bf16[64,7168]{1,0:T(8,128)(2,1)S(1)} %copy-done, s32[]{:T(128)S(6)} %select_n.7, s32[8,64]{1,0:T(8,128)S(1)} %copy.33, pred[8,64]{1,0:T(8,128)(4,1)S(1)} %bitcast.19), kind=kOutput, calls=%fused_computation | convolution fusion | flops 74014720 | bytes 1381380 | tf_op jit(solution)/shard_map/mct,td->mcd/dot_general | solution.py:302
  2.6 1.4 %fusion.17 = (f32[64]{0:T(128)S(1)}, f32[64,32]{0,1:T(8,128)S(1)}) fusion(pred[64,32]{0,1:T(8,128)(4,1)S(1)} %fusion.10, bf16[64,7168]{1,0:T(8,128)(2,1)S(1)} %copy-done, bf16[7168,32]{0,1:T(8,128)(2,1)} %param.7), kind=kOutput, calls=%fused_computation.23 | convolution fusion | flops 29370304 | bytes 1386752 | tf_op jit(solution)/shard_map/dot_general | solution.py:286
  4.1 0.2 fusion.7
  4.2 0.2 copy.35
  4.4 0.7 pad.4.sendw
  5.1 53.6 %shard_map.64.hid = bf16[320,2048]{1,0:T(8,128)(2,1)} custom-call(bf16[8,40,1792]{2,1,0:T(8,128)(2,1)} %convolution_convert_fusion.send, bf16[8,40,128]{2,1,0:T(8,128)(2,1)} %pad.4.sendw, bf16[4,4,7,256,512]{4,3,2,1,0:T(8,128)(2,1)} %bitcast.22, bf16[4,4,7,256,512]{4,3,2,1,0:T(8,128)(2,1)} %bitcast.23), custom_call_target="tpu_custom_call" | custom-call | flops 18790481920 | bytes 58720256 | tf_op jit(solution)/shard_map/pallas_call | solution.py:311
  58.7 0.1 copy.36
  58.7 0.1 copy.37
  58.9 0.1 copy.38
  59.0 0.1 eq.49
  59.1 0.7 and_convert_fusion.back
  59.8 0.0 copy-start.1
  59.8 45.9 %shard_map.65 = bf16[64,1792]{1,0:T(8,128)(2,1)} custom-call(bf16[320,2048]{1,0:T(8,128)(2,1)} %shard_map.64.hid, bf16[2048,7168]{1,0:T(8,128)(2,1)} %bitcast.24, bf16[64,320]{1,0:T(8,128)(2,1)} %and_convert_fusion.back), custom_call_target="tpu_custom_call" | custom-call | flops 9395240960 | bytes 29360128 | tf_op jit(solution)/shard_map/pallas_call | solution.py:336
  105.7 1.6 %copy.42 = bf16[64,1792]{1,0:T(8,128)(2,1)} copy(bf16[64,1792]{1,0:T(8,128)(2,1)} %shard_map.65) | data formatting | bytes 458752
  107.4 0.0 copy-done.1
  (8 shorter events, 0.1 us)
Async XLA Ops:
  0.0 1.2 %copy-start = (bf16[64,7168]{1,0:T(8,128)(2,1)S(1)}, bf16[64,7168]{1,0:T(8,128)(2,1)}, u32[]{:S(2)}) copy-start(bf16[64,7168]{1,0:T(8,128)(2,1)} %param.6) | copy-start | bytes 2752516
  59.8 47.6 %copy-start.1 = (bf16[64,7168]{1,0:T(8,128)(2,1)S(1)}, bf16[64,7168]{1,0:T(8,128)(2,1)}, u32[]{:S(2)}) copy-start(bf16[64,7168]{1,0:T(8,128)(2,1)} %param.6) | copy-start | bytes 2752516
